TPU v7x, 32 devices: a whole 2x2x4 slice. The times are simulated.
32 devices in a mesh: zone: 2 (over y), tile: 16 (over z, x, core).
Axes of the slice: x: 2, y: 2, z: 4, core: 2. Of those that a mesh axis runs over, the one named last changes fastest.
Arguments:
- tiles: bfloat16 [96, 13, 256, 256], P(('zone', 'tile')), may hold values from -6 to 6
- seam_list: int32 [64], P(('zone', 'tile')), may hold values from 0 to 2, as said below
- source: int32 [768], P('zone'), may hold values from 0 to 47, as said below
- offsets: int32 [768, 2], P('zone'), may hold values from -2 to 2
- fractions: float32 [768, 2], P('zone'), may hold values from 0 to 1
- blend: float32 [768], P('zone'), may hold values from 0.25 to 0.75
Outputs:
- polar_blocks: bfloat16 [768, 13, 128, 128], P(('zone', 'tile'))
Inputs may be any that keep to these rules, and one draw needn't show every extreme that they name: Within the blocks of one owner device, no source device (index v // 3 of the strip) supplies more than 3 blocks; in every draw each owner takes exactly 3 blocks from some source device. Source devices are unevenly popular. `seam_list`: the 2 entries of one device are distinct.
All inputs are finite; a program needn't handle non-finite values.
Results may differ from a plain program's by a relative error of at most 0.0062.
Values may be sent and summed in bfloat16 or wider, within the bound.
A program may use at most 192 MiB of HBM per device.

v0:
```python
import jax
import jax.numpy as jnp
from jax import lax
from jax.sharding import PartitionSpec as P

batch_slots = 8


def passed_along(value, axis, steps):
    count = lax.axis_size(axis)
    initial, last = (max(0, -steps), min(count, count - steps))
    return lax.ppermute(value, axis, [(source, source + steps) for source in range(initial, last)])


def cubic_weight(dist):
    mag = jnp.abs(dist)
    near = (1.5 * mag - 2.5) * mag * mag + 1.0
    far = ((-0.5 * mag + 2.5) * mag - 4.0) * mag + 2.0
    return jnp.where(mag <= 1.0, near, jnp.where(mag < 2.0, far, jnp.zeros_like(mag)))


def kernel_matrix(out_len, in_len, shift):
    rows = jnp.arange(out_len, dtype=jnp.float32)[:, None]
    cols = jnp.arange(in_len, dtype=jnp.float32)[None, :]
    return cubic_weight(cols - (2.0 * rows + shift)).astype(jnp.bfloat16)


def resample(mixed, offset_pair, fraction_pair):
    height = mixed.shape[1]
    width = mixed.shape[2]
    row_kernel = kernel_matrix(
        height // 2, height, offset_pair[0].astype(jnp.float32) + fraction_pair[0]
    )
    col_kernel = kernel_matrix(
        width // 2, width, offset_pair[1].astype(jnp.float32) + fraction_pair[1]
    )
    across = jnp.einsum(
        "bkt,ot->bko", mixed, col_kernel, preferred_element_type=jnp.float32
    ).astype(jnp.bfloat16)
    result = jnp.einsum("ik,bko->bio", row_kernel, across, preferred_element_type=jnp.float32)
    return result.astype(jnp.bfloat16)


def local(tiles, seam_list, source, offsets, fractions, blend):
    tile_count = lax.axis_size("tile")
    myself = lax.axis_index("tile")
    zone_index = lax.axis_index("zone")
    local_count = tiles.shape[0]
    per_owner = source.shape[0] // tile_count
    capacity = max(2, 2 * per_owner // tile_count)
    slots = tile_count * capacity
    block_shape = (tiles.shape[1], tiles.shape[2] // 2, tiles.shape[3] // 2)
    src_device = (source // local_count).reshape(tile_count, per_owner)
    order_ids = jnp.arange(per_owner, dtype=jnp.int32)
    same_device = src_device[:, :, None] == src_device[:, None, :]
    earlier = order_ids[None, :] < order_ids[:, None]
    rank = jnp.sum((same_device & earlier[None]).astype(jnp.int32), axis=2)
    wanted = (src_device[:, None, :] == myself) & (
        rank[:, None, :] == jnp.arange(capacity, dtype=jnp.int32)[None, :, None]
    )
    slot_block = jnp.sum(wanted.astype(jnp.int32) * order_ids, axis=2).reshape(slots)
    slot_owner = jnp.arange(slots, dtype=jnp.int32) // capacity
    slot_index = slot_owner * per_owner + slot_block
    picked = tiles[seam_list]
    near_tiles, near_list = passed_along((picked, seam_list), "zone", 1)

    def neighbour(index):
        match = near_list == index
        position = jnp.sum(
            match.astype(jnp.int32) * jnp.arange(near_list.shape[0], dtype=jnp.int32)
        )
        return (near_tiles[position], jnp.any(match))

    has_left = (zone_index > 0).astype(jnp.float32)

    def render(slot):
        block_index = slot_index[slot]
        local_tile = source[block_index] % local_count
        other, flagged = neighbour(local_tile)
        weight = blend[block_index] * flagged.astype(jnp.float32) * has_left
        primary = tiles[local_tile]
        mixed = (
            (1.0 - weight) * primary.astype(jnp.float32) + weight * other.astype(jnp.float32)
        ).astype(jnp.bfloat16)
        return resample(mixed, offsets[block_index], fractions[block_index])

    render_group = jax.vmap(render)
    groups = jnp.arange(slots, dtype=jnp.int32).reshape(slots // batch_slots, batch_slots)
    outgoing = lax.map(render_group, groups).reshape((slots,) + block_shape)
    incoming = lax.all_to_all(
        outgoing.reshape((tile_count, capacity) + block_shape),
        "tile",
        split_axis=0,
        concat_axis=0,
        tiled=True,
    )
    pick = src_device[myself] * capacity + rank[myself]
    return incoming.reshape((slots,) + block_shape)[pick]


def solution(mesh):
    in_specs = (
        P(("zone", "tile"), None, None, None),
        P(("zone", "tile")),
        P("zone"),
        P("zone", None),
        P("zone", None),
        P("zone"),
    )
    out_specs = P(("zone", "tile"), None, None, None)
    return jax.shard_map(local, mesh=mesh, in_specs=in_specs, out_specs=out_specs, check_vma=False)
```

profile of v0, /device:TPU:15, one launch (start us, length us, event | category | flops | bytes accessed | tf_op | source)
XLA Modules:
  0.0 792.0 jit_solution(14597977841447518665)
XLA Ops:
  0.7 5.0 gather_fusion.7
  10.4 1.5 copy.14
  13.5 68.8 %collective-permute-done = s32[2]{0:T(128)S(1)} collective-permute-done((s32[2]{0:T(128)}, s32[2]{0:T(128)S(1)}, u32[]{:S(2)}, u32[]{:S(2)}) %collective-permute-start) | collective-permute-done | bytes 40 | tf_op jit(solution)/shard_map/ppermute | solution.py:12
  82.3 220.9 %while.13 = (s32[]{:T(128)}, bf16[6,8,13,128,128]{3,4,2,1,0:T(8,128)(2,1)}, s32[2]{0:T(128)S(1)}, s32[6,8]{1,0:T(8,128)S(1)}, s32[48]{0:T(128)S(1)}, /*index=5*/...) while((s32[]{:T(128)}, ...), condition=%wide.region_5.6_spmd, body=%wide.region_2.5_spmd.sunk | while | flops 2672693760 | bytes 85231104 | solution.py:89
  83.0 1.5 gather_fusion.5
  87.8 6.6 gather_fusion.2
  94.4 9.4 %gather_fusion.3 = bf16[8,13,256,256]{3,2,1,0:T(8,128)(2,1)} fusion(bf16[3,13,256,256]{3,2,1,0:T(8,128)(2,1)} %get-tuple-element.394, s32[8]{0:T(128)S(1)} %get-tuple-element.352), kind=kCustom, calls=%fused_computation.3.clone.1 | custom fusion | bytes 27263104 | tf_op jit(solution)/shard_map/while/body/eval_jaxpr/vmap()/gather | solution.py:81
  104.5 14.8 %bitcast_dynamic-update-slice_fusion.2 = bf16[6,8,13,128,128]{3,4,2,1,0:T(8,128)(2,1)} fusion(bf16[6,8,13,128,128]{3,4,2,1,0:T(8,128)(2,1)} %get-tuple-element.374, s32[]{:T(128)} %get-tuple-element.373, bf16[8,13,256,256]{3,2,1,0:T(8,128)(2,1)} %gather_fusion.2, bf16[8,13,256,256]{3,2,1,0:T(8,128)(2,1)} %gather_fusion.3, ...), kind=kOutput, calls=%fused_computation.18.clone.1 | convolution fusion | flops 2672689152 | bytes 30679616 | tf_op jit(solution)/shard_map/while/body/eval_jaxpr/vmap(ik,bko->bio)/dot_general | solution.py:40
  120.0 1.5 gather_fusion.5
  124.8 6.4 gather_fusion.2
  131.2 9.0 %gather_fusion.3 = bf16[8,13,256,256]{3,2,1,0:T(8,128)(2,1)} fusion(bf16[3,13,256,256]{3,2,1,0:T(8,128)(2,1)} %get-tuple-element.394, s32[8]{0:T(128)S(1)} %get-tuple-element.352), kind=kCustom, calls=%fused_computation.3.clone.1 | custom fusion | bytes 27263104 | tf_op jit(solution)/shard_map/while/body/eval_jaxpr/vmap()/gather | solution.py:81
  141.0 14.9 %bitcast_dynamic-update-slice_fusion.2 = bf16[6,8,13,128,128]{3,4,2,1,0:T(8,128)(2,1)} fusion(bf16[6,8,13,128,128]{3,4,2,1,0:T(8,128)(2,1)} %get-tuple-element.374, s32[]{:T(128)} %get-tuple-element.373, bf16[8,13,256,256]{3,2,1,0:T(8,128)(2,1)} %gather_fusion.2, bf16[8,13,256,256]{3,2,1,0:T(8,128)(2,1)} %gather_fusion.3, ...), kind=kOutput, calls=%fused_computation.18.clone.1 | convolution fusion | flops 2672689152 | bytes 30679616 | tf_op jit(solution)/shard_map/while/body/eval_jaxpr/vmap(ik,bko->bio)/dot_general | solution.py:40
  156.6 1.5 gather_fusion.5
  161.4 6.6 gather_fusion.2
  168.0 9.3 %gather_fusion.3 = bf16[8,13,256,256]{3,2,1,0:T(8,128)(2,1)} fusion(bf16[3,13,256,256]{3,2,1,0:T(8,128)(2,1)} %get-tuple-element.394, s32[8]{0:T(128)S(1)} %get-tuple-element.352), kind=kCustom, calls=%fused_computation.3.clone.1 | custom fusion | bytes 27263104 | tf_op jit(solution)/shard_map/while/body/eval_jaxpr/vmap()/gather | solution.py:81
  178.0 14.9 %bitcast_dynamic-update-slice_fusion.2 = bf16[6,8,13,128,128]{3,4,2,1,0:T(8,128)(2,1)} fusion(bf16[6,8,13,128,128]{3,4,2,1,0:T(8,128)(2,1)} %get-tuple-element.374, s32[]{:T(128)} %get-tuple-element.373, bf16[8,13,256,256]{3,2,1,0:T(8,128)(2,1)} %gather_fusion.2, bf16[8,13,256,256]{3,2,1,0:T(8,128)(2,1)} %gather_fusion.3, ...), kind=kOutput, calls=%fused_computation.18.clone.1 | convolution fusion | flops 2672689152 | bytes 30679616 | tf_op jit(solution)/shard_map/while/body/eval_jaxpr/vmap(ik,bko->bio)/dot_general | solution.py:40
  193.6 1.5 gather_fusion.5
  198.4 6.7 gather_fusion.2
  205.1 9.3 %gather_fusion.3 = bf16[8,13,256,256]{3,2,1,0:T(8,128)(2,1)} fusion(bf16[3,13,256,256]{3,2,1,0:T(8,128)(2,1)} %get-tuple-element.394, s32[8]{0:T(128)S(1)} %get-tuple-element.352), kind=kCustom, calls=%fused_computation.3.clone.1 | custom fusion | bytes 27263104 | tf_op jit(solution)/shard_map/while/body/eval_jaxpr/vmap()/gather | solution.py:81
  215.2 14.9 %bitcast_dynamic-update-slice_fusion.2 = bf16[6,8,13,128,128]{3,4,2,1,0:T(8,128)(2,1)} fusion(bf16[6,8,13,128,128]{3,4,2,1,0:T(8,128)(2,1)} %get-tuple-element.374, s32[]{:T(128)} %get-tuple-element.373, bf16[8,13,256,256]{3,2,1,0:T(8,128)(2,1)} %gather_fusion.2, bf16[8,13,256,256]{3,2,1,0:T(8,128)(2,1)} %gather_fusion.3, ...), kind=kOutput, calls=%fused_computation.18.clone.1 | convolution fusion | flops 2672689152 | bytes 30679616 | tf_op jit(solution)/shard_map/while/body/eval_jaxpr/vmap(ik,bko->bio)/dot_general | solution.py:40
  230.8 1.5 gather_fusion.5
  235.6 6.4 gather_fusion.2
  241.9 9.3 %gather_fusion.3 = bf16[8,13,256,256]{3,2,1,0:T(8,128)(2,1)} fusion(bf16[3,13,256,256]{3,2,1,0:T(8,128)(2,1)} %get-tuple-element.394, s32[8]{0:T(128)S(1)} %get-tuple-element.352), kind=kCustom, calls=%fused_computation.3.clone.1 | custom fusion | bytes 27263104 | tf_op jit(solution)/shard_map/while/body/eval_jaxpr/vmap()/gather | solution.py:81
  252.0 14.8 %bitcast_dynamic-update-slice_fusion.2 = bf16[6,8,13,128,128]{3,4,2,1,0:T(8,128)(2,1)} fusion(bf16[6,8,13,128,128]{3,4,2,1,0:T(8,128)(2,1)} %get-tuple-element.374, s32[]{:T(128)} %get-tuple-element.373, bf16[8,13,256,256]{3,2,1,0:T(8,128)(2,1)} %gather_fusion.2, bf16[8,13,256,256]{3,2,1,0:T(8,128)(2,1)} %gather_fusion.3, ...), kind=kOutput, calls=%fused_computation.18.clone.1 | convolution fusion | flops 2672689152 | bytes 30679616 | tf_op jit(solution)/shard_map/while/body/eval_jaxpr/vmap(ik,bko->bio)/dot_general | solution.py:40
  267.5 1.5 gather_fusion.5
  272.3 6.4 gather_fusion.2
  278.6 8.9 %gather_fusion.3 = bf16[8,13,256,256]{3,2,1,0:T(8,128)(2,1)} fusion(bf16[3,13,256,256]{3,2,1,0:T(8,128)(2,1)} %get-tuple-element.394, s32[8]{0:T(128)S(1)} %get-tuple-element.352), kind=kCustom, calls=%fused_computation.3.clone.1 | custom fusion | bytes 27263104 | tf_op jit(solution)/shard_map/while/body/eval_jaxpr/vmap()/gather | solution.py:81
  288.3 14.8 %bitcast_dynamic-update-slice_fusion.2 = bf16[6,8,13,128,128]{3,4,2,1,0:T(8,128)(2,1)} fusion(bf16[6,8,13,128,128]{3,4,2,1,0:T(8,128)(2,1)} %get-tuple-element.374, s32[]{:T(128)} %get-tuple-element.373, bf16[8,13,256,256]{3,2,1,0:T(8,128)(2,1)} %gather_fusion.2, bf16[8,13,256,256]{3,2,1,0:T(8,128)(2,1)} %gather_fusion.3, ...), kind=kOutput, calls=%fused_computation.18.clone.1 | convolution fusion | flops 2672689152 | bytes 30679616 | tf_op jit(solution)/shard_map/while/body/eval_jaxpr/vmap(ik,bko->bio)/dot_general | solution.py:40
  303.2 26.7 %copy.16 = bf16[16,3,13,128,128]{4,3,2,1,0:T(8,128)(2,1)} copy(bf16[16,3,13,128,128]{3,4,2,1,0:T(8,128)(2,1)} %bitcast.61) | data formatting | bytes 40894464 | tf_op jit(solution)/shard_map/reshape;reshape | solution.py:91
  329.9 8.2 %all-to-all-start = ((bf16[16,3,13,128,128]{4,3,2,1,0:T(8,128)(2,1)}), bf16[16,3,13,128,128]{4,3,2,1,0:T(8,128)(2,1)}, u32[]{:S(2)}, u32[]{:S(2)}) async-start(bf16[16,3,13,128,128]{4,3,2,1,0:T(8,128)(2,1)} %copy.16), calls=%async_computation | async-start | bytes 40894464 | tf_op jit(solution)/shard_map/all_to_all | solution.py:90
  338.8 440.1 %all-to-all-done = bf16[16,3,13,128,128]{4,3,2,1,0:T(8,128)(2,1)} async-done(((bf16[16,3,13,128,128]{4,3,2,1,0:T(8,128)(2,1)}), bf16[16,3,13,128,128]{4,3,2,1,0:T(8,128)(2,1)}, u32[]{:S(2)}, u32[]{:S(2)}) %all-to-all-start) | async-done | bytes 20447264 | tf_op jit(solution)/shard_map/all_to_all | solution.py:90
  778.8 13.1 %gather_fusion.8 = bf16[24,13,128,128]{3,2,1,0:T(8,128)(2,1)} fusion(bf16[48,13,128,128]{3,2,1,0:T(8,128)(2,1)} %bitcast.16, s32[1024]{0:T(1024)S(1)} %pad_clamp_fusion.2), kind=kCustom, calls=%fused_computation.8 | custom fusion | bytes 20447328 | tf_op jit(solution)/shard_map/gather | solution.py:98
  (131 shorter events, 35.6 us)
Async XLA Ops:
  5.6 76.7 %collective-permute-start.1 = (bf16[2,13,256,256]{3,2,1,0:T(8,128)(2,1)}, bf16[2,13,256,256]{3,2,1,0:T(8,128)(2,1)S(1)}, u32[]{:S(2)}, u32[]{:S(2)}) collective-permute-start(bf16[2,13,256,256]{3,2,1,0:T(8,128)(2,1)} %gather_fusion.7), channel_id=1, source_target_pairs={{0,16},{1,17},{2,18},{3,19},{4,20},{5,21},{6,22},{7,23},{8,24},{9,... | collective-permute-start | bytes 10223624 | tf_op jit(solution)/shard_map/ppermute | solution.py:12
  6.9 75.4 %collective-permute-start = (s32[2]{0:T(128)}, s32[2]{0:T(128)S(1)}, u32[]{:S(2)}, u32[]{:S(2)}) collective-permute-start(s32[2]{0:T(128)} %param.9), channel_id=1, source_target_pairs={{0,16},{1,17},{2,18},{3,19},{4,20},{5,21},{6,22},{7,23},{8,24},{9,... | collective-permute-start | bytes 32 | tf_op jit(solution)/shard_map/ppermute | solution.py:12
  9.0 73.3 %copy-start.1 = (s32[16,24]{1,0:T(8,128)}, s32[16,24]{1,0:T(8,128)S(1)}, u32[]{:S(2)}) copy-start(s32[16,24]{1,0:T(8,128)S(1)} %broadcast_in_dim_reshape.2) | copy-start | bytes 4612
  9.5 0.6 copy-start.2
  94.4 9.5 %copy-start = (f32[384]{0:T(512)S(1)}, f32[384]{0:T(512)}, u32[]{:S(2)}) copy-start(f32[384]{0:T(512)} %get-tuple-element.392) | copy-start | bytes 4612 | tf_op jit(solution)/shard_map/while
  131.2 9.1 %copy-start = (f32[384]{0:T(512)S(1)}, f32[384]{0:T(512)}, u32[]{:S(2)}) copy-start(f32[384]{0:T(512)} %get-tuple-element.392) | copy-start | bytes 4612 | tf_op jit(solution)/shard_map/while
  168.0 9.4 %copy-start = (f32[384]{0:T(512)S(1)}, f32[384]{0:T(512)}, u32[]{:S(2)}) copy-start(f32[384]{0:T(512)} %get-tuple-element.392) | copy-start | bytes 4612 | tf_op jit(solution)/shard_map/while
  205.1 9.4 %copy-start = (f32[384]{0:T(512)S(1)}, f32[384]{0:T(512)}, u32[]{:S(2)}) copy-start(f32[384]{0:T(512)} %get-tuple-element.392) | copy-start | bytes 4612 | tf_op jit(solution)/shard_map/while
  241.9 9.4 %copy-start = (f32[384]{0:T(512)S(1)}, f32[384]{0:T(512)}, u32[]{:S(2)}) copy-start(f32[384]{0:T(512)} %get-tuple-element.392) | copy-start | bytes 4612 | tf_op jit(solution)/shard_map/while
  278.6 9.0 %copy-start = (f32[384]{0:T(512)S(1)}, f32[384]{0:T(512)}, u32[]{:S(2)}) copy-start(f32[384]{0:T(512)} %get-tuple-element.392) | copy-start | bytes 4612 | tf_op jit(solution)/shard_map/while
  329.9 448.9 %all-to-all-start = ((bf16[16,3,13,128,128]{4,3,2,1,0:T(8,128)(2,1)}), bf16[16,3,13,128,128]{4,3,2,1,0:T(8,128)(2,1)}, u32[]{:S(2)}, u32[]{:S(2)}) async-start(bf16[16,3,13,128,128]{4,3,2,1,0:T(8,128)(2,1)} %copy.16), calls=%async_computation | async-start | bytes 40894464 | tf_op jit(solution)/shard_map/all_to_all | solution.py:90
where the time goes:
time: 794 us; the launch traced here: 792 us
  waiting for transfers between devices  509 us (64%)
  local copies, waits for them, and re-layouts  177 us (22%)
  matrix products  89.2 us (11%)
  starting transfers between devices  10.8 us (1%)
    all_to_all x1, waiting for transfers between devices, local(): lax.all_to_all(outgoing.reshape((tile_count, capacity) + block_shape), 't...  440 us
    dot_general x6, matrix products, resample(): jnp.einsum('ik,bko->bio', row_kernel, across, preferred_element_type=jnp....  89.2 us
    ppermute x2, waiting for transfers between devices, passed_along(): lax.ppermute(value, axis, [(source, source + steps) for source in range(i...  68.9 us
    gather x6, local copies, waits for them, and re-layouts, render(): primary = tiles[local_tile]  55.2 us
    gather x6, local copies, waits for them, and re-layouts, neighbour(): return (near_tiles[position], jnp.any(match))  39.1 us
    another operation x1, local copies, waits for them, and re-layouts, local(): outgoing.reshape((tile_count, capacity) + block_shape)  26.7 us
    gather x12, local copies, waits for them, and re-layouts, render(): return resample(mixed, offsets[block_index], fractions[block_index])  18.1 us
  transfers between devices with their start and end apart: 3, of which 2 were waited for; matrix products, arithmetic and copies ran while one was open for 1% of the time, Pallas kernels for 0%

commit v1 on v0

v1 whole, which is shorter than its diff:
```python
import functools

import jax
import jax.numpy as jnp
from jax import lax
from jax.experimental import pallas as pl
from jax.experimental.pallas import tpu as pltpu
from jax.sharding import PartitionSpec as P

lag = 2
MESH = pl.DeviceIdType.MESH


def line_length(count):
    best = 1
    for length in range(1, count + 1):
        if count % length == 0 and length * length <= count:
            best = length
    return best


def cubic_weight(dist):
    mag = jnp.abs(dist)
    near = (1.5 * mag - 2.5) * mag * mag + 1.0
    far = ((-0.5 * mag + 2.5) * mag - 4.0) * mag + 2.0
    return jnp.where(mag <= 1.0, near, jnp.where(mag < 2.0, far, jnp.zeros_like(mag)))


def exchange_kernel(
    sizes,
    prim_ref,
    sec_ref,
    weight_ref,
    shift_ref,
    tiles,
    planes,
    seams,
    incoming,
    row_k,
    col_k,
    plane_v,
    seam_v,
    out_v,
    z_send,
    z_recv,
    y_send,
    y_recv,
    x_send,
    x_recv,
    local_sem,
    own_sem,
):
    zones, line, groups, slots = sizes
    loc, bands, height, width = tiles.shape
    seam_count = seams.shape[2]
    zone = lax.axis_index("zone")
    myself = lax.axis_index("tile")
    place = myself // groups
    group = myself % groups

    def device(zone_at, place_at, group_at):
        return (zone_at, place_at * groups + group_at)

    has_up = place + 1 < line
    has_down = place >= 1
    has_next = zone + 1 < zones
    has_left = zone >= 1

    barrier = pltpu.get_barrier_semaphore()

    def greet(zone_at, place_at, group_at):
        pl.semaphore_signal(
            barrier, inc=1, device_id=device(zone_at, place_at, group_at), device_id_type=MESH
        )

    pl.when(has_up)(lambda: greet(zone, place + 1, group))
    pl.when(has_down)(lambda: greet(zone, place - 1, group))
    pl.when(has_next)(lambda: greet(zone + 1, place, group))
    pl.when(has_left)(lambda: greet(zone - 1, place, group))
    for step in range(1, groups):
        greet(zone, place, lax.rem(group + step, groups))
    greeted = (
        has_up.astype(jnp.int32)
        + has_down.astype(jnp.int32)
        + has_next.astype(jnp.int32)
        + has_left.astype(jnp.int32)
        + (groups - 1)
    )
    pl.semaphore_wait(barrier, greeted)

    def hop_copy(way, hop, band, first):
        source = place - hop if way == 0 else place + hop
        target = place + 1 if way == 0 else place - 1
        return pltpu.make_async_remote_copy(
            src_ref=tiles.at[:, band] if first else planes.at[band, source],
            dst_ref=planes.at[band, source],
            send_sem=z_send.at[way, hop, band],
            recv_sem=z_recv.at[way, hop, band],
            device_id=device(zone, target, group),
            device_id_type=MESH,
        )

    def hop_arrival(way, hop, band):
        source = place - hop - 1 if way == 0 else place + hop + 1
        return pltpu.make_async_remote_copy(
            src_ref=planes.at[band, source],
            dst_ref=planes.at[band, source],
            send_sem=z_send.at[way, hop, band],
            recv_sem=z_recv.at[way, hop, band],
            device_id=device(zone, place - 1 if way == 0 else place + 1, group),
            device_id_type=MESH,
        )

    def seam_copy(source, band, own):
        return pltpu.make_async_remote_copy(
            src_ref=tiles.at[pl.ds(0, seam_count), band]
            if own
            else planes.at[band, source, pl.ds(0, seam_count)],
            dst_ref=seams.at[band, source],
            send_sem=y_send.at[source, band],
            recv_sem=y_recv.at[source, band],
            device_id=device(zone + 1, place, group),
            device_id_type=MESH,
        )

    def seam_arrival(source, band):
        return pltpu.make_async_remote_copy(
            src_ref=seams.at[band, source],
            dst_ref=seams.at[band, source],
            send_sem=y_send.at[source, band],
            recv_sem=y_recv.at[source, band],
            device_id=device(zone - 1, place, group),
            device_id_type=MESH,
        )

    def block_copy(step, band):
        target = lax.rem(group + step, groups)
        return pltpu.make_async_remote_copy(
            src_ref=out_v.at[band % 2, target],
            dst_ref=incoming.at[group, :, band],
            send_sem=x_send.at[step, band],
            recv_sem=x_recv.at[step, band],
            device_id=device(zone, place, target),
            device_id_type=MESH,
        )

    def block_arrival(step, band):
        sender = lax.rem(group + groups - step, groups)
        return pltpu.make_async_remote_copy(
            src_ref=out_v.at[band % 2, sender],
            dst_ref=incoming.at[sender, :, band],
            send_sem=x_send.at[step, band],
            recv_sem=x_recv.at[step, band],
            device_id=device(zone, place, sender),
            device_id_type=MESH,
        )

    def own_copy(band):
        return pltpu.make_async_copy(
            out_v.at[band % 2, group], incoming.at[group, :, band], own_sem.at[band % 2]
        )

    def sends_to(way, hop):
        if way == 0:
            return has_up & (place - hop >= 0)
        return has_down & (place + hop < line)

    def arrives_by(way, hop):
        if way == 0:
            return place - hop - 1 >= 0
        return place + hop + 1 < line

    def advance(step):
        for hop in range(line):
            band = step - lag * hop

            @pl.when((band >= 0) & (band < bands))
            def _():
                if hop == 0:

                    @pl.when(has_next)
                    def _():
                        seam_copy(place, band, True).start()

                for way in (0, 1):
                    if hop > 0:

                        @pl.when(arrives_by(way, hop - 1))
                        def _():
                            hop_arrival(way, hop - 1, band).wait_recv()

                    if hop < line - 1:

                        @pl.when(sends_to(way, hop))
                        def _():
                            hop_copy(way, hop, band, hop == 0).start()

                    if hop > 0:

                        @pl.when(arrives_by(way, hop - 1) & has_next)
                        def _():
                            source = place - hop if way == 0 else place + hop
                            seam_copy(source, band, False).start()

    def build(slot, carry):
        rows = lax.broadcasted_iota(jnp.int32, (height // 2, height), 0).astype(jnp.float32)
        cols = lax.broadcasted_iota(jnp.int32, (height // 2, height), 1).astype(jnp.float32)
        row_k[slot] = cubic_weight(cols - (2.0 * rows + shift_ref[slot, 0])).astype(jnp.bfloat16)
        rows = lax.broadcasted_iota(jnp.int32, (width, width // 2), 1).astype(jnp.float32)
        cols = lax.broadcasted_iota(jnp.int32, (width, width // 2), 0).astype(jnp.float32)
        col_k[slot] = cubic_weight(cols - (2.0 * rows + shift_ref[slot, 1])).astype(jnp.bfloat16)
        return carry

    def render(band, blended):
        def one(index, carry):
            for owner in range(groups):
                slot = owner * slots + index
                mixed = plane_v[prim_ref[slot]]
                if blended:
                    weight = weight_ref[slot]
                    other = seam_v[sec_ref[slot]]
                    mixed = (
                        (1.0 - weight) * mixed.astype(jnp.float32)
                        + weight * other.astype(jnp.float32)
                    ).astype(jnp.bfloat16)
                across = jnp.dot(mixed, col_k[slot], preferred_element_type=jnp.float32)
                result = jnp.dot(
                    row_k[slot],
                    across.astype(jnp.bfloat16),
                    preferred_element_type=jnp.float32,
                )
                out_v[band % 2, owner, index] = result.astype(jnp.bfloat16)
            return carry

        lax.fori_loop(0, slots, one, 0)

    def fetch(source, band, own):
        return pltpu.make_async_copy(
            tiles.at[:, band] if own else planes.at[band, source],
            plane_v.at[pl.ds(source * loc, loc)],
            local_sem.at[source],
        )

    def fetch_seam(source, band):
        return pltpu.make_async_copy(
            seams.at[band, source],
            seam_v.at[pl.ds(source * seam_count, seam_count)],
            local_sem.at[line + source],
        )

    def compute(band):
        for source in range(line):
            pl.when(place == source)(lambda: fetch(source, band, True).start())
            pl.when(place != source)(lambda: fetch(source, band, False).start())

        @pl.when(has_left)
        def _():
            for source in range(line):
                seam_arrival(source, band).wait_recv()
                fetch_seam(source, band).start()

        @pl.when(band >= 2)
        def _():
            for step in range(1, groups):
                block_copy(step, band - 2).wait_send()
            own_copy(band - 2).wait()

        for source in range(line):
            fetch(source, band, False).wait()

        @pl.when(has_left)
        def _():
            for source in range(line):
                fetch_seam(source, band).wait()
            render(band, True)

        @pl.when(jnp.logical_not(has_left))
        def _():
            render(band, False)

        for step in range(1, groups):
            block_copy(step, band).start()
        own_copy(band).start()

    head = lag * (line - 1)
    for step in range(lag):
        advance(step)
    lax.fori_loop(0, groups * slots, build, 0)

    def turn(step, carry):
        advance(step)
        band = step - head - 1

        @pl.when(band >= 0)
        def _():
            compute(band)

        return carry

    lax.fori_loop(lag, bands + head + 1, turn, 0)

    def settle(band, carry):
        for way in (0, 1):
            for hop in range(line - 1):

                @pl.when(sends_to(way, hop))
                def _():
                    hop_copy(way, hop, band, hop == 0).wait_send()

        @pl.when(has_next)
        def _():
            for source in range(line):
                pl.when(place == source)(lambda: seam_copy(source, band, True).wait_send())
                pl.when(place != source)(lambda: seam_copy(source, band, False).wait_send())

        @pl.when(band >= bands - 2)
        def _():
            for step in range(1, groups):
                block_copy(step, band).wait_send()
            own_copy(band).wait()

        for step in range(1, groups):
            block_arrival(step, band).wait_recv()
        return carry

    lax.fori_loop(0, bands, settle, 0)


def pick_kernel(pick_ref, block_ref, out_ref):
    out_ref[...] = block_ref[...]


def local(zones, tile_count, tiles, seam_list, source, offsets, fractions, blend):
    myself = lax.axis_index("tile")
    zone = lax.axis_index("zone")
    loc, bands, height, width = tiles.shape
    seam_count = seam_list.shape[0]
    line = line_length(tile_count)
    groups = tile_count // line
    place = myself // groups
    group = myself % groups
    per_owner = source.shape[0] // tile_count
    capacity = max(2, 2 * per_owner // tile_count)
    slots = min(per_owner, line * capacity)

    tile_ids = jnp.arange(loc, dtype=jnp.int32)
    list_ids = jnp.arange(seam_count, dtype=jnp.int32)

    def positions(lists):
        match = lists[..., None, :] == tile_ids[:, None]
        listed = jnp.any(match, axis=-1)
        at = jnp.sum(match * list_ids, axis=-1)
        free = jnp.logical_not(listed).astype(jnp.int32)
        below = (tile_ids[None, :] < tile_ids[:, None]).astype(jnp.int32)
        earlier = jnp.sum(free[..., None, :] * below, axis=-1)
        return jnp.where(listed, at, seam_count + earlier), listed

    mine, _ = positions(seam_list)
    order = jnp.sum(jnp.where(mine[None, :] == tile_ids[:, None], tile_ids[None, :], 0), axis=1)
    arranged = tiles[order]

    lists = lax.all_gather(seam_list, ("zone", "tile"), axis=0, tiled=True)
    lists = lists.reshape(zones, line, groups, seam_count)
    here = lax.dynamic_index_in_dim(lists[:, :, :, :], zone, 0, keepdims=False)
    here = lax.dynamic_index_in_dim(here, group, 1, keepdims=False)
    left = lax.dynamic_index_in_dim(lists, jnp.maximum(zone - 1, 0), 0, keepdims=False)
    left = lax.dynamic_index_in_dim(left, group, 1, keepdims=False)
    here_at, _ = positions(here)
    left_at, left_listed = positions(left)

    def rows_of(array):
        array = array.reshape((line, groups, per_owner) + array.shape[1:])
        return lax.dynamic_index_in_dim(array, place, 0, keepdims=False)

    wanted = rows_of(source)
    device = wanted // loc
    from_group = device % groups
    from_place = device // groups
    tile = wanted % loc
    ids = jnp.arange(per_owner, dtype=jnp.int32)
    same = from_group[:, :, None] == from_group[:, None, :]
    rank = jnp.sum((same & (ids[None, :] < ids[:, None])[None]).astype(jnp.int32), axis=2)
    entry = from_place * loc + tile
    primary = from_place * loc + here_at.reshape(-1)[entry]
    flagged = left_listed.reshape(-1)[entry] & (zone > 0)
    second = from_place * seam_count + jnp.where(
        left_listed.reshape(-1)[entry], left_at.reshape(-1)[entry], 0
    )
    weight = rows_of(blend) * flagged.astype(jnp.float32)
    shift = rows_of(offsets.astype(jnp.float32) + fractions)

    taken = (from_group == group)[:, None, :] & (
        rank[:, None, :] == jnp.arange(slots, dtype=jnp.int32)[None, :, None]
    )
    held = jnp.sum(taken.astype(jnp.int32) * ids, axis=2)
    flat = (jnp.arange(groups, dtype=jnp.int32)[:, None] * per_owner + held).reshape(-1)
    primary = primary.reshape(-1)[flat]
    second = second.reshape(-1)[flat]
    weight = weight.reshape(-1)[flat]
    shift = shift.reshape(-1, 2)[flat]
    picks = lax.dynamic_index_in_dim(from_group * slots + rank, group, 0, keepdims=False)

    half = (height // 2, width // 2)
    total = groups * slots
    any_space = pl.BlockSpec(memory_space=pl.ANY)
    smem = pl.BlockSpec(memory_space=pltpu.SMEM)
    kind = tiles.dtype
    _, _, incoming = pl.pallas_call(
        functools.partial(exchange_kernel, (zones, line, groups, slots)),
        out_shape=[
            jax.ShapeDtypeStruct((bands, line, loc, height, width), kind),
            jax.ShapeDtypeStruct((bands, line, seam_count, height, width), kind),
            jax.ShapeDtypeStruct((groups, slots, bands) + half, kind),
        ],
        in_specs=[smem] * 4 + [any_space],
        out_specs=[any_space] * 3,
        scratch_shapes=[
            pltpu.VMEM((total, height // 2, height), kind),
            pltpu.VMEM((total, width, width // 2), kind),
            pltpu.VMEM((line * loc, height, width), kind),
            pltpu.VMEM((line * seam_count, height, width), kind),
            pltpu.VMEM((2, groups, slots) + half, kind),
            pltpu.SemaphoreType.DMA((2, line - 1, bands)),
            pltpu.SemaphoreType.DMA((2, line - 1, bands)),
            pltpu.SemaphoreType.DMA((line, bands)),
            pltpu.SemaphoreType.DMA((line, bands)),
            pltpu.SemaphoreType.DMA((groups, bands)),
            pltpu.SemaphoreType.DMA((groups, bands)),
            pltpu.SemaphoreType.DMA((2 * line,)),
            pltpu.SemaphoreType.DMA((2,)),
        ],
        compiler_params=pltpu.CompilerParams(
            collective_id=0, has_side_effects=True, vmem_limit_bytes=40 * 1024 * 1024
        ),
    )(primary, second, weight, shift, arranged)

    incoming = incoming.reshape((total, bands) + half)
    return pl.pallas_call(
        pick_kernel,
        grid_spec=pltpu.PrefetchScalarGridSpec(
            num_scalar_prefetch=1,
            grid=(per_owner,),
            in_specs=[
                pl.BlockSpec((1, bands) + half, lambda block, pick: (pick[block], 0, 0, 0))
            ],
            out_specs=pl.BlockSpec((1, bands) + half, lambda block, pick: (block, 0, 0, 0)),
        ),
        out_shape=jax.ShapeDtypeStruct((per_owner, bands) + half, kind),
    )(picks, incoming)


def solution(mesh):
    in_specs = (
        P(("zone", "tile"), None, None, None),
        P(("zone", "tile")),
        P("zone"),
        P("zone", None),
        P("zone", None),
        P("zone"),
    )
    out_specs = P(("zone", "tile"), None, None, None)
    body = functools.partial(local, mesh.shape["zone"], mesh.shape["tile"])
    return jax.shard_map(body, mesh=mesh, in_specs=in_specs, out_specs=out_specs, check_vma=False)
```

time: 794 us -> 485 us (0.61)
  the two profiles are of different devices: /device:TPU:15 before, /device:TPU:5 now
where the time goes in v1:
time: 485 us; the launch traced here: 484 us
  Pallas kernels  421 us (87%)
  blocking collectives  39.6 us (8%)
  local copies, waits for them, and re-layouts  19.7 us (4%)
    pallas_call x1, Pallas kernels, local(): pl.pallas_call(functools.partial(exchange_kernel, (zones, line, groups, s...  404 us
    unnamed x1, blocking collectives  39.6 us
    pallas_call x1, Pallas kernels, local(): pl.pallas_call(pick_kernel, grid_spec=pltpu.PrefetchScalarGridSpec(num_sc...  16.8 us

profile of v1, /device:TPU:5, one launch (start us, length us, event | category | flops | bytes accessed | tf_op | source)
XLA Modules:
  0.0 483.8 jit_solution(6257143858531182998)
XLA Ops:
  0.0 0.7 fusion.10
  0.8 0.1 select_reduce_fusion.4
  0.9 0.7 select_reduce_fusion.5
  1.6 0.1 select_reduce_fusion.3
  1.8 0.9 dynamic-update-slice
  2.6 39.6 %all-reduce = s32[64]{0:T(128)S(1)} all-reduce(s32[64]{0:T(128)S(1)} %dynamic-update-slice), channel_id=1, replica_groups=mesh['zone'=2,'tile'=16] {'zone','tile'}, use_global_device_ids=true, to_apply=%add | all-reduce | flops 64 | bytes 512
  42.2 0.7 convert_add_fusion
  42.9 0.8 reshape.346
  43.8 0.2 convert_reduce_fusion
  44.2 0.5 fusion.11.pick_ref
  44.7 0.3 select_reduce_fusion
  45.0 0.1 copy.32
  45.3 0.8 reshape.349
  46.2 0.1 reshape.347
  46.3 0.1 copy.33
  46.4 0.1 copy.41
  46.6 1.2 gather_fusion.2
  47.9 0.8 gather_fusion.5
  48.7 0.1 copy.35
  49.0 0.1 copy.40
  49.1 0.1 copy.31
  49.2 0.2 multiply_reduce_fusion
  49.6 1.2 gather_fusion.3
  50.8 0.8 gather_fusion.4
  51.8 1.2 gather_fusion
  53.1 0.8 gather_fusion.1
  53.8 0.1 copy.39
  54.0 0.6 gather_fusion.6
  54.6 5.8 %gather_fusion.7 = bf16[3,13,256,256]{3,2,1,0:T(8,128)(2,1)} fusion(bf16[3,13,256,256]{3,2,1,0:T(8,128)(2,1)} %param.6, s32[1024]{0:T(1024)S(1)} %pad_clamp_fusion), kind=kCustom, calls=%fused_computation.7 | custom fusion | bytes 10223628 | tf_op jit(solution)/shard_map/gather | solution.py:360
  60.4 2.4 copy-done
  62.8 404.2 %shard_map.64 = (bf16[13,4,3,256,256]{4,3,2,1,0:T(8,128)(2,1)}, bf16[13,4,2,256,256]{4,3,2,1,0:T(8,128)(2,1)}, bf16[4,12,13,128,128]{4,3,2,1,0:T(8,128)(2,1)}) custom-call(s32[48]{0:T(128)S(1)} %gather_fusion.1, s32[48]{0:T(128)S(1)} %gather_fusion.4, f32[48]{0:T(128)S(1)} %gather_fusion.5, f32[48,2]{1,0:T(8,128)S(1)} %gather_fusion.6, ...), custom_call_target="tpu_custom_call" | custom-call | tf_op jit(solution)/shard_map/pallas_call | solution.py:408
  467.1 16.8 %shard_map.65 = bf16[24,13,128,128]{3,2,1,0:T(8,128)(2,1)} custom-call(s32[24]{0:T(128)} %fusion.11.pick_ref, bf16[48,13,128,128]{3,2,1,0:T(8,128)(2,1)} %bitcast.45), custom_call_target="tpu_custom_call" | custom-call | tf_op jit(solution)/shard_map/pallas_call | solution.py:438
  (42 shorter events, 1.4 us)
Async XLA Ops:
  60.4 2.4 copy-start

commit v2 on v1

--- a/solution.py
+++ b/solution.py
@@ -1,4 +1,5 @@
 import functools
+import math
 
 import jax
 import jax.numpy as jnp
@@ -28,11 +29,13 @@
 
 def exchange_kernel(
     sizes,
-    prim_ref,
-    sec_ref,
-    weight_ref,
+    from_ref,
+    tile_ref,
+    blend_ref,
     shift_ref,
-    tiles,
+    order_ref,
+    card_ref,
+    tiles_hbm,
     planes,
     seams,
     incoming,
@@ -41,6 +44,15 @@
     plane_v,
     seam_v,
     out_v,
+    raw_v,
+    tiles,
+    cards_v,
+    cards,
+    prim_ref,
+    sec_ref,
+    weight_ref,
+    card_send,
+    card_recv,
     z_send,
     z_recv,
     y_send,
@@ -51,7 +63,7 @@
     own_sem,
 ):
     zones, line, groups, slots = sizes
-    loc, bands, height, width = tiles.shape
+    bands, loc, height, width = tiles.shape
     seam_count = seams.shape[2]
     zone = lax.axis_index("zone")
     myself = lax.axis_index("tile")
@@ -66,6 +78,11 @@
     has_next = zone + 1 < zones
     has_left = zone >= 1
 
+    raw_copy = pltpu.make_async_copy(tiles_hbm, raw_v, own_sem.at[0])
+    raw_copy.start()
+    cards_v[...] = jnp.zeros_like(cards_v)
+    cards_v[0, place] = card_ref[...]
+
     barrier = pltpu.get_barrier_semaphore()
 
     def greet(zone_at, place_at, group_at):
@@ -73,26 +90,55 @@
             barrier, inc=1, device_id=device(zone_at, place_at, group_at), device_id_type=MESH
         )
 
-    pl.when(has_up)(lambda: greet(zone, place + 1, group))
-    pl.when(has_down)(lambda: greet(zone, place - 1, group))
-    pl.when(has_next)(lambda: greet(zone + 1, place, group))
-    pl.when(has_left)(lambda: greet(zone - 1, place, group))
+    for other in range(line):
+        pl.when(place != other)(lambda: greet(zone, other, group))
+        pl.when(has_next)(lambda: greet(zone + 1, other, group))
+        pl.when(has_left)(lambda: greet(zone - 1, other, group))
     for step in range(1, groups):
         greet(zone, place, lax.rem(group + step, groups))
+
+    raw_copy.wait()
+
+    def arrange(band, carry):
+        for spot in range(loc):
+            tiles[band, spot] = raw_v[order_ref[spot], band]
+        return carry
+
+    lax.fori_loop(0, bands, arrange, 0)
     greeted = (
-        has_up.astype(jnp.int32)
-        + has_down.astype(jnp.int32)
-        + has_next.astype(jnp.int32)
-        + has_left.astype(jnp.int32)
-        + (groups - 1)
+        line * (has_next.astype(jnp.int32) + has_left.astype(jnp.int32)) + (line - 1) + (groups - 1)
     )
     pl.semaphore_wait(barrier, greeted)
+
+    def card_copy(later, other):
+        return pltpu.make_async_remote_copy(
+            src_ref=card_ref,
+            dst_ref=cards_v.at[later, place],
+            send_sem=card_send.at[later, other],
+            recv_sem=card_recv.at[later, place],
+            device_id=device(zone + later, other, group),
+            device_id_type=MESH,
+        )
+
+    def card_arrival(later, sender):
+        return pltpu.make_async_remote_copy(
+            src_ref=card_ref,
+            dst_ref=cards_v.at[later, sender],
+            send_sem=card_send.at[later, sender],
+            recv_sem=card_recv.at[later, sender],
+            device_id=device(zone - later, sender, group),
+            device_id_type=MESH,
+        )
+
+    for other in range(line):
+        pl.when(place != other)(lambda: card_copy(0, other).start())
+        pl.when(has_next)(lambda: card_copy(1, other).start())
 
     def hop_copy(way, hop, band, first):
         source = place - hop if way == 0 else place + hop
         target = place + 1 if way == 0 else place - 1
         return pltpu.make_async_remote_copy(
-            src_ref=tiles.at[:, band] if first else planes.at[band, source],
+            src_ref=tiles.at[band] if first else planes.at[band, source],
             dst_ref=planes.at[band, source],
             send_sem=z_send.at[way, hop, band],
             recv_sem=z_recv.at[way, hop, band],
@@ -113,7 +159,7 @@
 
     def seam_copy(source, band, own):
         return pltpu.make_async_remote_copy(
-            src_ref=tiles.at[pl.ds(0, seam_count), band]
+            src_ref=tiles.at[band, pl.ds(0, seam_count)]
             if own
             else planes.at[band, source, pl.ds(0, seam_count)],
             dst_ref=seams.at[band, source],
@@ -203,40 +249,72 @@
                             seam_copy(source, band, False).start()
 
     def build(slot, carry):
+        origin = from_ref[slot]
+        tile = tile_ref[slot]
+        listed, spot, below, flagged, second = 0, 0, 0, 0, 0
+        for entry in range(seam_count):
+            here = cards[0, origin, 0, entry]
+            left = cards[1, origin, 0, entry]
+            listed = listed + jnp.where(here == tile, 1, 0)
+            spot = spot + jnp.where(here == tile, entry, 0)
+            below = below + jnp.where(here < tile, 1, 0)
+            flagged = flagged + jnp.where(left == tile, 1, 0)
+            second = second + jnp.where(left == tile, entry, 0)
+        spot = jnp.where(listed > 0, spot, seam_count + tile - below)
+        prim_ref[slot] = origin * loc + spot
+        sec_ref[slot] = origin * seam_count + second
+        weight_ref[slot] = jnp.where(flagged > 0, blend_ref[slot], 0.0)
         rows = lax.broadcasted_iota(jnp.int32, (height // 2, height), 0).astype(jnp.float32)
         cols = lax.broadcasted_iota(jnp.int32, (height // 2, height), 1).astype(jnp.float32)
-        row_k[slot] = cubic_weight(cols - (2.0 * rows + shift_ref[slot, 0])).astype(jnp.bfloat16)
+        row_k[slot] = cubic_weight(cols - (2.0 * rows + shift_ref[2 * slot])).astype(jnp.bfloat16)
         rows = lax.broadcasted_iota(jnp.int32, (width, width // 2), 1).astype(jnp.float32)
         cols = lax.broadcasted_iota(jnp.int32, (width, width // 2), 0).astype(jnp.float32)
-        col_k[slot] = cubic_weight(cols - (2.0 * rows + shift_ref[slot, 1])).astype(jnp.bfloat16)
-        return carry
+        col_k[slot] = cubic_weight(cols - (2.0 * rows + shift_ref[2 * slot + 1])).astype(jnp.bfloat16)
+        return carry
+
+    together = math.gcd(slots, 4)
 
     def render(band, blended):
-        def one(index, carry):
-            for owner in range(groups):
-                slot = owner * slots + index
-                mixed = plane_v[prim_ref[slot]]
+        def part(owner, index, carry):
+            spots = [index * together + more for more in range(together)]
+            mixed = []
+            for spot in spots:
+                slot = owner * slots + spot
+                pixels = plane_v[prim_ref[slot]]
                 if blended:
                     weight = weight_ref[slot]
                     other = seam_v[sec_ref[slot]]
-                    mixed = (
-                        (1.0 - weight) * mixed.astype(jnp.float32)
+                    pixels = (
+                        (1.0 - weight) * pixels.astype(jnp.float32)
                         + weight * other.astype(jnp.float32)
                     ).astype(jnp.bfloat16)
-                across = jnp.dot(mixed, col_k[slot], preferred_element_type=jnp.float32)
-                result = jnp.dot(
-                    row_k[slot],
-                    across.astype(jnp.bfloat16),
-                    preferred_element_type=jnp.float32,
-                )
-                out_v[band % 2, owner, index] = result.astype(jnp.bfloat16)
+                mixed.append(pixels)
+            across = [
+                jnp.dot(
+                    pixels, col_k[owner * slots + spot], preferred_element_type=jnp.float32
+                ).astype(jnp.bfloat16)
+                for spot, pixels in zip(spots, mixed)
+            ]
+            results = [
+                jnp.dot(row_k[owner * slots + spot], value, preferred_element_type=jnp.float32)
+                for spot, value in zip(spots, across)
+            ]
+            for spot, result in zip(spots, results):
+                out_v[band % 2, owner, spot] = result.astype(jnp.bfloat16)
             return carry
 
-        lax.fori_loop(0, slots, one, 0)
+        def one_owner(step, carry):
+            owner = lax.rem(group + step, groups)
+            lax.fori_loop(0, slots // together, functools.partial(part, owner), 0)
+            pl.when(step < groups)(lambda: block_copy(step, band).start())
+            pl.when(step == groups)(lambda: own_copy(band).start())
+            return carry
+
+        lax.fori_loop(1, groups + 1, one_owner, 0)
 
     def fetch(source, band, own):
         return pltpu.make_async_copy(
-            tiles.at[:, band] if own else planes.at[band, source],
+            tiles.at[band] if own else planes.at[band, source],
             plane_v.at[pl.ds(source * loc, loc)],
             local_sem.at[source],
         )
@@ -278,18 +356,20 @@
         def _():
             render(band, False)
 
-        for step in range(1, groups):
-            block_copy(step, band).start()
-        own_copy(band).start()
-
     head = lag * (line - 1)
     for step in range(lag):
         advance(step)
+    for sender in range(line):
+        pl.when(place != sender)(lambda: card_arrival(0, sender).wait_recv())
+        pl.when(has_left)(lambda: card_arrival(1, sender).wait_recv())
+    cards_copy = pltpu.make_async_copy(cards_v, cards, own_sem.at[0])
+    cards_copy.start()
+    cards_copy.wait()
     lax.fori_loop(0, groups * slots, build, 0)
 
     def turn(step, carry):
         advance(step)
-        band = step - head - 1
+        band = step - head
 
         @pl.when(band >= 0)
         def _():
@@ -297,7 +377,11 @@
 
         return carry
 
-    lax.fori_loop(lag, bands + head + 1, turn, 0)
+    lax.fori_loop(lag, bands + head, turn, 0)
+
+    for other in range(line):
+        pl.when(place != other)(lambda: card_copy(0, other).wait_send())
+        pl.when(has_next)(lambda: card_copy(1, other).wait_send())
 
     def settle(band, carry):
         for way in (0, 1):
@@ -326,85 +410,127 @@
     lax.fori_loop(0, bands, settle, 0)
 
 
-def pick_kernel(pick_ref, block_ref, out_ref):
-    out_ref[...] = block_ref[...]
+def table_kernel(
+    sizes,
+    seam_ref,
+    source_ref,
+    shift_ref,
+    blend_ref,
+    from_ref,
+    tile_ref,
+    weight_ref,
+    moved_ref,
+    pick_ref,
+    order_ref,
+    card_ref,
+    counts,
+):
+    line, groups, slots, loc, per_owner = sizes
+    seam_count = seam_ref.shape[0]
+    myself = lax.axis_index("tile")
+    place = myself // groups
+    group = myself % groups
+
+    def clear(slot, carry):
+        from_ref[slot] = 0
+        tile_ref[slot] = 0
+        weight_ref[slot] = 0.0
+        moved_ref[2 * slot] = 0.0
+        moved_ref[2 * slot + 1] = 0.0
+        return carry
+
+    lax.fori_loop(0, groups * slots + 1, clear, 0)
+
+    for owner in range(groups):
+
+        def fill(index, count):
+            block = (place * groups + owner) * per_owner + index
+            value = source_ref[block]
+            device = value // loc
+            slot = owner * slots + count
+            from_ref[slot] = device // groups
+            tile_ref[slot] = value - device * loc
+            weight_ref[slot] = blend_ref[block]
+            moved_ref[2 * slot] = shift_ref[2 * block]
+            moved_ref[2 * slot + 1] = shift_ref[2 * block + 1]
+            return count + jnp.where(lax.rem(device, groups) == group, 1, 0)
+
+        lax.fori_loop(0, per_owner, fill, 0)
+
+    for sender in range(groups):
+        counts[sender] = 0
+
+    def choose(index, carry):
+        sender = lax.rem(source_ref[myself * per_owner + index] // loc, groups)
+        count = counts[sender]
+        pick_ref[index] = sender * slots + count
+        counts[sender] = count + 1
+        return carry
+
+    lax.fori_loop(0, per_owner, choose, 0)
+
+    columns = lax.broadcasted_iota(jnp.int32, card_ref.shape, 1)
+    card = jnp.zeros(card_ref.shape, jnp.int32)
+    for entry in range(seam_count):
+        card = jnp.where(columns == entry, seam_ref[entry], card)
+    card_ref[...] = card
+    for tile in range(loc):
+        listed, spot, below = 0, 0, 0
+        for entry in range(seam_count):
+            listed = listed + jnp.where(seam_ref[entry] == tile, 1, 0)
+            spot = spot + jnp.where(seam_ref[entry] == tile, entry, 0)
+            below = below + jnp.where(seam_ref[entry] < tile, 1, 0)
+        order_ref[jnp.where(listed > 0, spot, seam_count + tile - below)] = tile
+
+
+def pick_kernel(pick_ref, incoming, out, sems):
+    def copy(block):
+        return pltpu.make_async_copy(incoming.at[pick_ref[block]], out.at[block], sems.at[block])
+
+    def begin(block, carry):
+        copy(block).start()
+        return carry
+
+    def finish(block, carry):
+        copy(block).wait()
+        return carry
+
+    lax.fori_loop(0, out.shape[0], begin, 0)
+    lax.fori_loop(0, out.shape[0], finish, 0)
 
 
 def local(zones, tile_count, tiles, seam_list, source, offsets, fractions, blend):
-    myself = lax.axis_index("tile")
-    zone = lax.axis_index("zone")
     loc, bands, height, width = tiles.shape
     seam_count = seam_list.shape[0]
     line = line_length(tile_count)
     groups = tile_count // line
-    place = myself // groups
-    group = myself % groups
     per_owner = source.shape[0] // tile_count
     capacity = max(2, 2 * per_owner // tile_count)
     slots = min(per_owner, line * capacity)
-
-    tile_ids = jnp.arange(loc, dtype=jnp.int32)
-    list_ids = jnp.arange(seam_count, dtype=jnp.int32)
-
-    def positions(lists):
-        match = lists[..., None, :] == tile_ids[:, None]
-        listed = jnp.any(match, axis=-1)
-        at = jnp.sum(match * list_ids, axis=-1)
-        free = jnp.logical_not(listed).astype(jnp.int32)
-        below = (tile_ids[None, :] < tile_ids[:, None]).astype(jnp.int32)
-        earlier = jnp.sum(free[..., None, :] * below, axis=-1)
-        return jnp.where(listed, at, seam_count + earlier), listed
-
-    mine, _ = positions(seam_list)
-    order = jnp.sum(jnp.where(mine[None, :] == tile_ids[:, None], tile_ids[None, :], 0), axis=1)
-    arranged = tiles[order]
-
-    lists = lax.all_gather(seam_list, ("zone", "tile"), axis=0, tiled=True)
-    lists = lists.reshape(zones, line, groups, seam_count)
-    here = lax.dynamic_index_in_dim(lists[:, :, :, :], zone, 0, keepdims=False)
-    here = lax.dynamic_index_in_dim(here, group, 1, keepdims=False)
-    left = lax.dynamic_index_in_dim(lists, jnp.maximum(zone - 1, 0), 0, keepdims=False)
-    left = lax.dynamic_index_in_dim(left, group, 1, keepdims=False)
-    here_at, _ = positions(here)
-    left_at, left_listed = positions(left)
-
-    def rows_of(array):
-        array = array.reshape((line, groups, per_owner) + array.shape[1:])
-        return lax.dynamic_index_in_dim(array, place, 0, keepdims=False)
-
-    wanted = rows_of(source)
-    device = wanted // loc
-    from_group = device % groups
-    from_place = device // groups
-    tile = wanted % loc
-    ids = jnp.arange(per_owner, dtype=jnp.int32)
-    same = from_group[:, :, None] == from_group[:, None, :]
-    rank = jnp.sum((same & (ids[None, :] < ids[:, None])[None]).astype(jnp.int32), axis=2)
-    entry = from_place * loc + tile
-    primary = from_place * loc + here_at.reshape(-1)[entry]
-    flagged = left_listed.reshape(-1)[entry] & (zone > 0)
-    second = from_place * seam_count + jnp.where(
-        left_listed.reshape(-1)[entry], left_at.reshape(-1)[entry], 0
-    )
-    weight = rows_of(blend) * flagged.astype(jnp.float32)
-    shift = rows_of(offsets.astype(jnp.float32) + fractions)
-
-    taken = (from_group == group)[:, None, :] & (
-        rank[:, None, :] == jnp.arange(slots, dtype=jnp.int32)[None, :, None]
-    )
-    held = jnp.sum(taken.astype(jnp.int32) * ids, axis=2)
-    flat = (jnp.arange(groups, dtype=jnp.int32)[:, None] * per_owner + held).reshape(-1)
-    primary = primary.reshape(-1)[flat]
-    second = second.reshape(-1)[flat]
-    weight = weight.reshape(-1)[flat]
-    shift = shift.reshape(-1, 2)[flat]
-    picks = lax.dynamic_index_in_dim(from_group * slots + rank, group, 0, keepdims=False)
-
     half = (height // 2, width // 2)
     total = groups * slots
     any_space = pl.BlockSpec(memory_space=pl.ANY)
     smem = pl.BlockSpec(memory_space=pltpu.SMEM)
+    vmem = pl.BlockSpec(memory_space=pltpu.VMEM)
     kind = tiles.dtype
+
+    shift = (offsets.astype(jnp.float32) + fractions).reshape(-1)
+    came, tile, weight, moved, picks, order, card = pl.pallas_call(
+        functools.partial(table_kernel, (line, groups, slots, loc, per_owner)),
+        out_shape=[
+            jax.ShapeDtypeStruct((total + 1,), jnp.int32),
+            jax.ShapeDtypeStruct((total + 1,), jnp.int32),
+            jax.ShapeDtypeStruct((total + 1,), jnp.float32),
+            jax.ShapeDtypeStruct((2 * total + 2,), jnp.float32),
+            jax.ShapeDtypeStruct((per_owner,), jnp.int32),
+            jax.ShapeDtypeStruct((loc,), jnp.int32),
+            jax.ShapeDtypeStruct((8, 128), jnp.int32),
+        ],
+        in_specs=[smem] * 4,
+        out_specs=[smem] * 6 + [vmem],
+        scratch_shapes=[pltpu.SMEM((groups,), jnp.int32)],
+    )(seam_list, source, shift, blend)
+
     _, _, incoming = pl.pallas_call(
         functools.partial(exchange_kernel, (zones, line, groups, slots)),
         out_shape=[
@@ -412,7 +538,7 @@
             jax.ShapeDtypeStruct((bands, line, seam_count, height, width), kind),
             jax.ShapeDtypeStruct((groups, slots, bands) + half, kind),
         ],
-        in_specs=[smem] * 4 + [any_space],
+        in_specs=[smem] * 5 + [vmem, any_space],
         out_specs=[any_space] * 3,
         scratch_shapes=[
             pltpu.VMEM((total, height // 2, height), kind),
@@ -420,6 +546,15 @@
             pltpu.VMEM((line * loc, height, width), kind),
             pltpu.VMEM((line * seam_count, height, width), kind),
             pltpu.VMEM((2, groups, slots) + half, kind),
+            pltpu.VMEM((loc, bands, height, width), kind),
+            pltpu.VMEM((bands, loc, height, width), kind),
+            pltpu.VMEM((2, line, 8, 128), jnp.int32),
+            pltpu.SMEM((2, line, 8, 128), jnp.int32),
+            pltpu.SMEM((total,), jnp.int32),
+            pltpu.SMEM((total,), jnp.int32),
+            pltpu.SMEM((total,), jnp.float32),
+            pltpu.SemaphoreType.DMA((2, line)),
+            pltpu.SemaphoreType.DMA((2, line)),
             pltpu.SemaphoreType.DMA((2, line - 1, bands)),
             pltpu.SemaphoreType.DMA((2, line - 1, bands)),
             pltpu.SemaphoreType.DMA((line, bands)),
@@ -430,23 +565,17 @@
             pltpu.SemaphoreType.DMA((2,)),
         ],
         compiler_params=pltpu.CompilerParams(
-            collective_id=0, has_side_effects=True, vmem_limit_bytes=40 * 1024 * 1024
+            collective_id=0, has_side_effects=True, vmem_limit_bytes=48 * 1024 * 1024
         ),
-    )(primary, second, weight, shift, arranged)
-
-    incoming = incoming.reshape((total, bands) + half)
+    )(came, tile, weight, moved, order, card, tiles)
+
     return pl.pallas_call(
         pick_kernel,
-        grid_spec=pltpu.PrefetchScalarGridSpec(
-            num_scalar_prefetch=1,
-            grid=(per_owner,),
-            in_specs=[
-                pl.BlockSpec((1, bands) + half, lambda block, pick: (pick[block], 0, 0, 0))
-            ],
-            out_specs=pl.BlockSpec((1, bands) + half, lambda block, pick: (block, 0, 0, 0)),
-        ),
+        in_specs=[smem, any_space],
+        out_specs=any_space,
         out_shape=jax.ShapeDtypeStruct((per_owner, bands) + half, kind),
-    )(picks, incoming)
+        scratch_shapes=[pltpu.SemaphoreType.DMA((per_owner,))],
+    )(picks, incoming.reshape((total, bands) + half))
 
 
 def solution(mesh):

time: 485 us -> 707 us (1.46)
  Pallas kernels: 421 us -> 698 us
  blocking collectives: 39.6 us -> 0 us
  local copies, waits for them, and re-layouts: 19.7 us -> 7.17 us
    pallas_call x1 -> x2, Pallas kernels: 16.8 us -> 316 us  [the longest x1 312 us: local(): pl.pallas_call(pick_kernel, in_specs=[smem, any_space], out_specs=any_spa...]
    unnamed x1 -> x0, blocking collectives: 39.6 us -> none
    pallas_call x1, Pallas kernels: 404 us -> 382 us  [local(): pl.pallas_call(functools.partial(exchange_kernel, (zones, line, groups, s...]
    gather x8 -> x0, local copies, waits for them, and re-layouts: 12.4 us -> none  [the longest x1 5.8 us: local(): arranged = tiles[order]]
where the time goes in v2:
time: 707 us; the launch traced here: 706 us
  Pallas kernels  698 us (99%)
  local copies, waits for them, and re-layouts  7.17 us (1%)
    pallas_call x1, Pallas kernels, local(): pl.pallas_call(functools.partial(exchange_kernel, (zones, line, groups, s...  382 us
    pallas_call x1, Pallas kernels, local(): pl.pallas_call(pick_kernel, in_specs=[smem, any_space], out_specs=any_spa...  312 us

profile of v2, /device:TPU:5, one launch (start us, length us, event | category | flops | bytes accessed | tf_op | source)
XLA Modules:
  0.0 706.3 jit_solution(8791864934781809591)
XLA Ops:
  0.0 0.7 convert_add_fusion
  0.7 0.1 copy.7
  0.9 0.7 reshape.6.shift_ref
  1.6 4.7 shard_map.64
  6.3 0.0 copy-start
  6.3 2.4 copy-done
  8.7 0.0 copy-start.1
  8.7 0.7 copy-done.1
  9.4 0.0 copy-start.2
  9.4 0.7 copy-done.2
  10.1 0.0 copy-start.3
  10.1 0.6 copy-done.3
  10.7 0.0 copy-start.4
  10.7 0.7 copy-done.4
  11.4 0.0 copy-start.5
  11.4 0.6 copy-done.5
  12.0 0.0 copy-start.6
  12.0 0.6 copy-done.6
  12.6 382.0 %shard_map.65 = (bf16[13,4,3,256,256]{4,3,2,1,0:T(8,128)(2,1)}, bf16[13,4,2,256,256]{4,3,2,1,0:T(8,128)(2,1)}, bf16[4,12,13,128,128]{4,3,2,1,0:T(8,128)(2,1)}) custom-call(s32[49]{0:T(128)S(1)} %copy-done.2, s32[49]{0:T(128)S(1)} %copy-done.3, f32[49]{0:T(128)S(1)} %copy-done.4, f32[98]{0:T(128)S(1)} %copy-done.5, s32[3]{0:T(128)S(1)} %copy-done.6, ...), custom_call_target="tpu_custom_call" | custom-call | tf_op jit(solution)/shard_map/pallas_call | solution.py:534
  394.6 311.7 %shard_map.66 = bf16[24,13,128,128]{3,2,1,0:T(8,128)(2,1)} custom-call(s32[24]{0:T(128)} %get-tuple-element.13.pick_ref, bf16[48,13,128,128]{3,2,1,0:T(8,128)(2,1)} %bitcast.1), custom_call_target="tpu_custom_call" | custom-call | tf_op jit(solution)/shard_map/pallas_call | solution.py:572
Async XLA Ops:
  6.3 2.5 copy-start
  8.7 0.7 copy-start.1
  9.4 0.7 copy-start.2
  10.1 0.6 copy-start.3
  10.7 0.7 copy-start.4
  11.4 0.6 copy-start.5
  12.0 0.6 copy-start.6

commit v3 on v2

--- a/solution.py
+++ b/solution.py
@@ -8,6 +8,7 @@
 from jax.experimental.pallas import tpu as pltpu
 from jax.sharding import PartitionSpec as P
 
+pair = 2
 lag = 2
 MESH = pl.DeviceIdType.MESH
 
@@ -35,7 +36,7 @@
     shift_ref,
     order_ref,
     card_ref,
-    tiles_hbm,
+    raw_v,
     planes,
     seams,
     incoming,
@@ -44,7 +45,6 @@
     plane_v,
     seam_v,
     out_v,
-    raw_v,
     tiles,
     cards_v,
     cards,
@@ -78,8 +78,6 @@
     has_next = zone + 1 < zones
     has_left = zone >= 1
 
-    raw_copy = pltpu.make_async_copy(tiles_hbm, raw_v, own_sem.at[0])
-    raw_copy.start()
     cards_v[...] = jnp.zeros_like(cards_v)
     cards_v[0, place] = card_ref[...]
 
@@ -97,7 +95,6 @@
     for step in range(1, groups):
         greet(zone, place, lax.rem(group + step, groups))
 
-    raw_copy.wait()
 
     def arrange(band, carry):
         for spot in range(loc):
@@ -179,11 +176,17 @@
             device_id_type=MESH,
         )
 
+    chunks = incoming.shape[2] // pair
+    spare = incoming.shape[2] - bands
+
+    def landing(owner, chunk):
+        return incoming.at[owner, :, pl.ds(chunk * pair, pair)]
+
     def block_copy(step, band):
         target = lax.rem(group + step, groups)
         return pltpu.make_async_remote_copy(
             src_ref=out_v.at[band % 2, target],
-            dst_ref=incoming.at[group, :, band],
+            dst_ref=landing(group, band),
             send_sem=x_send.at[step, band],
             recv_sem=x_recv.at[step, band],
             device_id=device(zone, place, target),
@@ -194,7 +197,7 @@
         sender = lax.rem(group + groups - step, groups)
         return pltpu.make_async_remote_copy(
             src_ref=out_v.at[band % 2, sender],
-            dst_ref=incoming.at[sender, :, band],
+            dst_ref=landing(sender, band),
             send_sem=x_send.at[step, band],
             recv_sem=x_recv.at[step, band],
             device_id=device(zone, place, sender),
@@ -203,7 +206,7 @@
 
     def own_copy(band):
         return pltpu.make_async_copy(
-            out_v.at[band % 2, group], incoming.at[group, :, band], own_sem.at[band % 2]
+            out_v.at[band % 2, group], landing(group, band), own_sem.at[band % 2]
         )
 
     def sends_to(way, hop):
@@ -272,7 +275,7 @@
         col_k[slot] = cubic_weight(cols - (2.0 * rows + shift_ref[2 * slot + 1])).astype(jnp.bfloat16)
         return carry
 
-    together = math.gcd(slots, 4)
+    together = math.gcd(slots, 2)
 
     def render(band, blended):
         def part(owner, index, carry):
@@ -280,15 +283,18 @@
             mixed = []
             for spot in spots:
                 slot = owner * slots + spot
-                pixels = plane_v[prim_ref[slot]]
-                if blended:
-                    weight = weight_ref[slot]
-                    other = seam_v[sec_ref[slot]]
-                    pixels = (
-                        (1.0 - weight) * pixels.astype(jnp.float32)
-                        + weight * other.astype(jnp.float32)
-                    ).astype(jnp.bfloat16)
-                mixed.append(pixels)
+                parts = []
+                for half in range(pair):
+                    pixels = plane_v[half, prim_ref[slot]]
+                    if blended:
+                        weight = weight_ref[slot]
+                        other = seam_v[half, sec_ref[slot]]
+                        pixels = (
+                            (1.0 - weight) * pixels.astype(jnp.float32)
+                            + weight * other.astype(jnp.float32)
+                        ).astype(jnp.bfloat16)
+                    parts.append(pixels)
+                mixed.append(jnp.concatenate(parts, axis=0))
             across = [
                 jnp.dot(
                     pixels, col_k[owner * slots + spot], preferred_element_type=jnp.float32
@@ -296,11 +302,21 @@
                 for spot, pixels in zip(spots, mixed)
             ]
             results = [
-                jnp.dot(row_k[owner * slots + spot], value, preferred_element_type=jnp.float32)
+                jnp.dot(
+                    row_k[owner * slots + spot],
+                    jnp.concatenate(
+                        [value[half * height : (half + 1) * height] for half in range(pair)],
+                        axis=1,
+                    ),
+                    preferred_element_type=jnp.float32,
+                ).astype(jnp.bfloat16)
                 for spot, value in zip(spots, across)
             ]
             for spot, result in zip(spots, results):
-                out_v[band % 2, owner, spot] = result.astype(jnp.bfloat16)
+                for half in range(pair):
+                    out_v[band % 2, owner, spot, half] = result[
+                        :, half * (width // 2) : (half + 1) * (width // 2)
+                    ]
             return carry
 
         def one_owner(step, carry):
@@ -312,49 +328,61 @@
 
         lax.fori_loop(1, groups + 1, one_owner, 0)
 
-    def fetch(source, band, own):
+    def fetch(source, band, half, own):
         return pltpu.make_async_copy(
             tiles.at[band] if own else planes.at[band, source],
-            plane_v.at[pl.ds(source * loc, loc)],
-            local_sem.at[source],
-        )
-
-    def fetch_seam(source, band):
+            plane_v.at[half, pl.ds(source * loc, loc)],
+            local_sem.at[half, source],
+        )
+
+    def fetch_seam(source, band, half):
         return pltpu.make_async_copy(
             seams.at[band, source],
-            seam_v.at[pl.ds(source * seam_count, seam_count)],
-            local_sem.at[line + source],
-        )
-
-    def compute(band):
-        for source in range(line):
-            pl.when(place == source)(lambda: fetch(source, band, True).start())
-            pl.when(place != source)(lambda: fetch(source, band, False).start())
+            seam_v.at[half, pl.ds(source * seam_count, seam_count)],
+            local_sem.at[half, line + source],
+        )
+
+    def compute(chunk):
+        real = [chunk * pair - spare + half for half in range(pair)]
+        used = [jnp.maximum(band, 0) for band in real]
+        for half in range(pair):
+            for source in range(line):
+                pl.when(place == source)(lambda: fetch(source, used[half], half, True).start())
+                pl.when(place != source)(lambda: fetch(source, used[half], half, False).start())
 
         @pl.when(has_left)
         def _():
-            for source in range(line):
-                seam_arrival(source, band).wait_recv()
-                fetch_seam(source, band).start()
-
-        @pl.when(band >= 2)
+            for half in range(pair):
+
+                @pl.when(real[half] >= 0)
+                def _():
+                    for source in range(line):
+                        seam_arrival(source, used[half]).wait_recv()
+
+            for half in range(pair):
+                for source in range(line):
+                    fetch_seam(source, used[half], half).start()
+
+        @pl.when(chunk >= 2)
         def _():
             for step in range(1, groups):
-                block_copy(step, band - 2).wait_send()
-            own_copy(band - 2).wait()
-
-        for source in range(line):
-            fetch(source, band, False).wait()
+                block_copy(step, chunk - 2).wait_send()
+            own_copy(chunk - 2).wait()
+
+        for half in range(pair):
+            for source in range(line):
+                fetch(source, used[half], half, False).wait()
 
         @pl.when(has_left)
         def _():
-            for source in range(line):
-                fetch_seam(source, band).wait()
-            render(band, True)
+            for half in range(pair):
+                for source in range(line):
+                    fetch_seam(source, used[half], half).wait()
+            render(chunk, True)
 
         @pl.when(jnp.logical_not(has_left))
         def _():
-            render(band, False)
+            render(chunk, False)
 
     head = lag * (line - 1)
     for step in range(lag):
@@ -369,11 +397,11 @@
 
     def turn(step, carry):
         advance(step)
-        band = step - head
-
-        @pl.when(band >= 0)
+        done = step - head + 1 + spare
+
+        @pl.when((step >= head) & (done % pair == 0))
         def _():
-            compute(band)
+            compute(done // pair - 1)
 
         return carry
 
@@ -397,17 +425,22 @@
                 pl.when(place == source)(lambda: seam_copy(source, band, True).wait_send())
                 pl.when(place != source)(lambda: seam_copy(source, band, False).wait_send())
 
-        @pl.when(band >= bands - 2)
+        return carry
+
+    lax.fori_loop(0, bands, settle, 0)
+
+    def gather_in(chunk, carry):
+        @pl.when(chunk >= chunks - 2)
         def _():
             for step in range(1, groups):
-                block_copy(step, band).wait_send()
-            own_copy(band).wait()
+                block_copy(step, chunk).wait_send()
+            own_copy(chunk).wait()
 
         for step in range(1, groups):
-            block_arrival(step, band).wait_recv()
-        return carry
-
-    lax.fori_loop(0, bands, settle, 0)
+            block_arrival(step, chunk).wait_recv()
+        return carry
+
+    lax.fori_loop(0, chunks, gather_in, 0)
 
 
 def table_kernel(
@@ -483,19 +516,34 @@
         order_ref[jnp.where(listed > 0, spot, seam_count + tile - below)] = tile
 
 
-def pick_kernel(pick_ref, incoming, out, sems):
-    def copy(block):
-        return pltpu.make_async_copy(incoming.at[pick_ref[block]], out.at[block], sems.at[block])
+def pick_kernel(pick_ref, incoming, out, held, in_sems, out_sems):
+    spare = incoming.shape[1] - out.shape[1]
+
+    def copy_in(block):
+        return pltpu.make_async_copy(
+            incoming.at[pick_ref[block], pl.ds(spare, out.shape[1])],
+            held.at[block],
+            in_sems.at[block],
+        )
+
+    def copy_out(block):
+        return pltpu.make_async_copy(held.at[block], out.at[block], out_sems.at[block])
 
     def begin(block, carry):
-        copy(block).start()
+        copy_in(block).start()
+        return carry
+
+    def relay(block, carry):
+        copy_in(block).wait()
+        copy_out(block).start()
         return carry
 
     def finish(block, carry):
-        copy(block).wait()
+        copy_out(block).wait()
         return carry
 
     lax.fori_loop(0, out.shape[0], begin, 0)
+    lax.fori_loop(0, out.shape[0], relay, 0)
     lax.fori_loop(0, out.shape[0], finish, 0)
 
 
@@ -509,6 +557,7 @@
     slots = min(per_owner, line * capacity)
     half = (height // 2, width // 2)
     total = groups * slots
+    padded = -(-bands // pair) * pair
     any_space = pl.BlockSpec(memory_space=pl.ANY)
     smem = pl.BlockSpec(memory_space=pltpu.SMEM)
     vmem = pl.BlockSpec(memory_space=pltpu.VMEM)
@@ -536,17 +585,16 @@
         out_shape=[
             jax.ShapeDtypeStruct((bands, line, loc, height, width), kind),
             jax.ShapeDtypeStruct((bands, line, seam_count, height, width), kind),
-            jax.ShapeDtypeStruct((groups, slots, bands) + half, kind),
+            jax.ShapeDtypeStruct((groups, slots, padded) + half, kind),
         ],
-        in_specs=[smem] * 5 + [vmem, any_space],
+        in_specs=[smem] * 5 + [vmem, vmem],
         out_specs=[any_space] * 3,
         scratch_shapes=[
             pltpu.VMEM((total, height // 2, height), kind),
             pltpu.VMEM((total, width, width // 2), kind),
-            pltpu.VMEM((line * loc, height, width), kind),
-            pltpu.VMEM((line * seam_count, height, width), kind),
-            pltpu.VMEM((2, groups, slots) + half, kind),
-            pltpu.VMEM((loc, bands, height, width), kind),
+            pltpu.VMEM((pair, line * loc, height, width), kind),
+            pltpu.VMEM((pair, line * seam_count, height, width), kind),
+            pltpu.VMEM((2, groups, slots, pair) + half, kind),
             pltpu.VMEM((bands, loc, height, width), kind),
             pltpu.VMEM((2, line, 8, 128), jnp.int32),
             pltpu.SMEM((2, line, 8, 128), jnp.int32),
@@ -559,13 +607,13 @@
             pltpu.SemaphoreType.DMA((2, line - 1, bands)),
             pltpu.SemaphoreType.DMA((line, bands)),
             pltpu.SemaphoreType.DMA((line, bands)),
-            pltpu.SemaphoreType.DMA((groups, bands)),
-            pltpu.SemaphoreType.DMA((groups, bands)),
-            pltpu.SemaphoreType.DMA((2 * line,)),
+            pltpu.SemaphoreType.DMA((groups, padded // pair)),
+            pltpu.SemaphoreType.DMA((groups, padded // pair)),
+            pltpu.SemaphoreType.DMA((pair, 2 * line)),
             pltpu.SemaphoreType.DMA((2,)),
         ],
         compiler_params=pltpu.CompilerParams(
-            collective_id=0, has_side_effects=True, vmem_limit_bytes=48 * 1024 * 1024
+            collective_id=0, has_side_effects=True, vmem_limit_bytes=52 * 1024 * 1024
         ),
     )(came, tile, weight, moved, order, card, tiles)
 
@@ -574,8 +622,13 @@
         in_specs=[smem, any_space],
         out_specs=any_space,
         out_shape=jax.ShapeDtypeStruct((per_owner, bands) + half, kind),
-        scratch_shapes=[pltpu.SemaphoreType.DMA((per_owner,))],
-    )(picks, incoming.reshape((total, bands) + half))
+        scratch_shapes=[
+            pltpu.VMEM((per_owner, bands) + half, kind),
+            pltpu.SemaphoreType.DMA((per_owner,)),
+            pltpu.SemaphoreType.DMA((per_owner,)),
+        ],
+        compiler_params=pltpu.CompilerParams(vmem_limit_bytes=32 * 1024 * 1024),
+    )(picks, incoming.reshape((total, padded) + half))
 
 
 def solution(mesh):

time: 707 us -> 431 us (0.61)
  Pallas kernels: 698 us -> 417 us
    pallas_call x1, Pallas kernels: 312 us -> 10.5 us  [local(): pl.pallas_call(pick_kernel, in_specs=[smem, any_space], out_specs=any_spa...]
    pallas_call x1, Pallas kernels: 382 us -> 402 us  [local(): pl.pallas_call(functools.partial(exchange_kernel, (zones, line, groups, s...]
where the time goes in v3:
time: 431 us; the launch traced here: 430 us
  Pallas kernels  417 us (97%)
  local copies, waits for them, and re-layouts  12.5 us (3%)
    pallas_call x1, Pallas kernels, local(): pl.pallas_call(functools.partial(exchange_kernel, (zones, line, groups, s...  402 us
    unnamed x16, local copies, waits for them, and re-layouts  11.7 us
    pallas_call x1, Pallas kernels, local(): pl.pallas_call(pick_kernel, in_specs=[smem, any_space], out_specs=any_spa...  10.5 us

profile of v3, /device:TPU:5, one launch (start us, length us, event | category | flops | bytes accessed | tf_op | source)
XLA Modules:
  0.0 430.4 jit_solution(1639595373462863071)
XLA Ops:
  0.0 0.7 convert_add_fusion
  0.7 0.1 copy.7
  0.9 0.7 reshape.6.shift_ref
  1.6 4.7 %shard_map.64 = (s32[49]{0:T(128)}, s32[49]{0:T(128)}, f32[49]{0:T(128)}, f32[98]{0:T(128)}, s32[24]{0:T(128)}, /*index=5*/s32[3]{0:T(128)}, s32[8,128]{1,0:T(8,128)}) custom-call(s32[2]{0:T(128)} %seam_ref.1, s32[384]{0:T(512)} %source_ref.1, f32[768]{0:T(1024)} %reshape.6.shift_ref, f32[384]{0:T(512)} %blend_ref.1), custom_call_target="tpu_custom_call" | custom-call | tf_op jit(solution)/shard_map/pallas_call | solution.py:567
  6.3 0.0 copy-start.1
  6.3 0.7 copy-done.1
  6.9 0.0 copy-start.3
  7.0 0.6 copy-done.3
  7.6 0.0 copy-start.4
  7.6 0.7 copy-done.4
  8.2 0.0 copy-start.5
  8.2 0.6 copy-done.5
  8.9 0.0 copy-start.6
  8.9 0.6 copy-done.6
  9.5 0.0 copy-start.7
  9.5 0.6 copy-done.7
  10.1 401.9 %shard_map.65 = (bf16[13,4,3,256,256]{4,3,2,1,0:T(8,128)(2,1)}, bf16[13,4,2,256,256]{4,3,2,1,0:T(8,128)(2,1)}, bf16[4,12,14,128,128]{4,3,2,1,0:T(8,128)(2,1)}) custom-call(s32[49]{0:T(128)S(1)} %copy-done.3, s32[49]{0:T(128)S(1)} %copy-done.4, f32[49]{0:T(128)S(1)} %copy-done.5, f32[98]{0:T(128)S(1)} %copy-done.6, s32[3]{0:T(128)S(1)} %copy-done.7, ...), custom_call_target="tpu_custom_call" | custom-call | tf_op jit(solution)/shard_map/pallas_call | solution.py:583
  412.0 0.0 copy-start
  412.0 7.3 %copy-done = bf16[4,12,14,128,128]{4,3,2,1,0:T(8,128)(2,1)S(1)} copy-done((bf16[4,12,14,128,128]{4,3,2,1,0:T(8,128)(2,1)S(1)}, bf16[4,12,14,128,128]{4,3,2,1,0:T(8,128)(2,1)}, u32[]{:S(2)}) %copy-start) | copy-done | bytes 22020120
  419.2 0.0 copy-start.2
  419.3 0.6 copy-done.2
  419.8 10.5 %shard_map.66 = bf16[24,13,128,128]{3,2,1,0:T(8,128)(2,1)} custom-call(s32[24]{0:T(128)S(1)} %copy-done.2, bf16[48,14,128,128]{3,2,1,0:T(8,128)(2,1)S(1)} %bitcast.1), custom_call_target="tpu_custom_call" | custom-call | tf_op jit(solution)/shard_map/pallas_call | solution.py:620
Async XLA Ops:
  6.3 0.7 copy-start.1
  6.9 0.6 copy-start.3
  7.6 0.7 copy-start.4
  8.2 0.6 copy-start.5
  8.9 0.6 copy-start.6
  9.5 0.6 copy-start.7
  412.0 7.3 %copy-start = (bf16[4,12,14,128,128]{4,3,2,1,0:T(8,128)(2,1)S(1)}, bf16[4,12,14,128,128]{4,3,2,1,0:T(8,128)(2,1)}, u32[]{:S(2)}) copy-start(bf16[4,12,14,128,128]{4,3,2,1,0:T(8,128)(2,1)} %get-tuple-element.20) | copy-start | bytes 66060292
  419.2 0.6 copy-start.2

commit v4 on v3

--- a/solution.py
+++ b/solution.py
@@ -8,8 +8,8 @@
 from jax.experimental.pallas import tpu as pltpu
 from jax.sharding import PartitionSpec as P
 
-pair = 2
-lag = 2
+pair = 1
+lead = 1
 MESH = pl.DeviceIdType.MESH
 
 
@@ -220,8 +220,8 @@
         return place + hop + 1 < line
 
     def advance(step):
-        for hop in range(line):
-            band = step - lag * hop
+        for hop in reversed(range(line)):
+            band = step - hop - (lead if hop > 0 else 0)
 
             @pl.when((band >= 0) & (band < bands))
             def _():
@@ -275,7 +275,7 @@
         col_k[slot] = cubic_weight(cols - (2.0 * rows + shift_ref[2 * slot + 1])).astype(jnp.bfloat16)
         return carry
 
-    together = math.gcd(slots, 2)
+    together = math.gcd(slots, 4)
 
     def render(band, blended):
         def part(owner, index, carry):
@@ -384,8 +384,8 @@
         def _():
             render(chunk, False)
 
-    head = lag * (line - 1)
-    for step in range(lag):
+    head = line - 1 + lead
+    for step in range(1 + lead):
         advance(step)
     for sender in range(line):
         pl.when(place != sender)(lambda: card_arrival(0, sender).wait_recv())
@@ -405,7 +405,7 @@
 
         return carry
 
-    lax.fori_loop(lag, bands + head, turn, 0)
+    lax.fori_loop(1 + lead, bands + head, turn, 0)
 
     for other in range(line):
         pl.when(place != other)(lambda: card_copy(0, other).wait_send())
@@ -627,7 +627,7 @@
             pltpu.SemaphoreType.DMA((per_owner,)),
             pltpu.SemaphoreType.DMA((per_owner,)),
         ],
-        compiler_params=pltpu.CompilerParams(vmem_limit_bytes=32 * 1024 * 1024),
+        compiler_params=pltpu.CompilerParams(vmem_limit_bytes=56 * 1024 * 1024),
     )(picks, incoming.reshape((total, padded) + half))
 
 

time: 431 us -> 391 us (0.907)
  Pallas kernels: 417 us -> 383 us
  local copies, waits for them, and re-layouts: 12.5 us -> 4.77 us
    pallas_call x1, Pallas kernels: 402 us -> 370 us  [local(): pl.pallas_call(functools.partial(exchange_kernel, (zones, line, groups, s...]
    unnamed x16 -> x12, local copies, waits for them, and re-layouts: 11.7 us -> 3.89 us
where the time goes in v4:
time: 391 us; the launch traced here: 389 us
  Pallas kernels  383 us (98%)
  local copies, waits for them, and re-layouts  4.77 us (1%)
    pallas_call x1, Pallas kernels, local(): pl.pallas_call(functools.partial(exchange_kernel, (zones, line, groups, s...  370 us
    pallas_call x1, Pallas kernels, local(): pl.pallas_call(pick_kernel, in_specs=[smem, any_space], out_specs=any_spa...  8.67 us

profile of v4, /device:TPU:5, one launch (start us, length us, event | category | flops | bytes accessed | tf_op | source)
XLA Modules:
  0.0 388.5 jit_solution(13543496727909839304)
XLA Ops:
  0.0 0.7 convert_add_fusion
  0.7 0.1 copy.7
  0.9 0.7 reshape.6.shift_ref
  1.6 4.7 %shard_map.64 = (s32[49]{0:T(128)}, s32[49]{0:T(128)}, f32[49]{0:T(128)}, f32[98]{0:T(128)}, s32[24]{0:T(128)}, /*index=5*/s32[3]{0:T(128)}, s32[8,128]{1,0:T(8,128)}) custom-call(s32[2]{0:T(128)} %seam_ref.1, s32[384]{0:T(512)} %source_ref.1, f32[768]{0:T(1024)} %reshape.6.shift_ref, f32[384]{0:T(512)} %blend_ref.1), custom_call_target="tpu_custom_call" | custom-call | tf_op jit(solution)/shard_map/pallas_call | solution.py:567
  6.3 0.0 copy-start
  6.3 0.7 copy-done
  6.9 0.0 copy-start.1
  7.0 0.7 copy-done.1
  7.6 0.0 copy-start.2
  7.6 0.7 copy-done.2
  8.3 0.0 copy-start.3
  8.3 0.6 copy-done.3
  8.9 0.0 copy-start.4
  8.9 0.7 copy-done.4
  9.6 0.0 copy-start.5
  9.6 0.6 copy-done.5
  10.2 369.7 %shard_map.65 = (bf16[13,4,3,256,256]{4,3,2,1,0:T(8,128)(2,1)}, bf16[13,4,2,256,256]{4,3,2,1,0:T(8,128)(2,1)}, bf16[4,12,13,128,128]{4,3,2,1,0:T(8,128)(2,1)}) custom-call(s32[49]{0:T(128)S(1)} %copy-done.1, s32[49]{0:T(128)S(1)} %copy-done.2, f32[49]{0:T(128)S(1)} %copy-done.3, f32[98]{0:T(128)S(1)} %copy-done.4, s32[3]{0:T(128)S(1)} %copy-done.5, ...), custom_call_target="tpu_custom_call" | custom-call | tf_op jit(solution)/shard_map/pallas_call | solution.py:583
  379.9 8.7 %shard_map.66 = bf16[24,13,128,128]{3,2,1,0:T(8,128)(2,1)} custom-call(s32[24]{0:T(128)} %get-tuple-element.13.pick_ref, bf16[48,13,128,128]{3,2,1,0:T(8,128)(2,1)} %bitcast.1), custom_call_target="tpu_custom_call" | custom-call | tf_op jit(solution)/shard_map/pallas_call | solution.py:620
Async XLA Ops:
  6.3 0.7 copy-start
  6.9 0.7 copy-start.1
  7.6 0.7 copy-start.2
  8.3 0.6 copy-start.3
  8.9 0.7 copy-start.4
  9.6 0.6 copy-start.5
